TPU v7x, 768 devices: a whole 4x8x12 slice. The times are simulated.
768 devices in a mesh: wide: 64 (over y, x, core), narrow: 12 (over z).
Axes of the slice: x: 4, y: 8, z: 12, core: 2. Of those that a mesh axis runs over, the one named last changes fastest.
Arguments:
- features: bfloat16 [393216, 256], P(('wide', 'narrow')), may hold values from -6 to 6
- upstream: bfloat16 [393216, 256], P(('wide', 'narrow')), may hold values from -6 to 6
- visit_counts: bfloat16 [1179648, 512], P(('wide', 'narrow')), may hold values from 0 to 8, as said below
- target_rows: int32 [768, 1536], P(('wide', 'narrow')), may hold values from 0 to 512, as said below
- message_weight: bfloat16 [2, 256, 256], replicated, may hold values from -0.375 to 0.375
- message_offset: float32 [2, 256], replicated, may hold values from -3 to 3
- self_weight: bfloat16 [2, 256, 256], replicated, may hold values from -0.375 to 0.375
- neighbor_weight: bfloat16 [2, 256, 256], replicated, may hold values from -0.375 to 0.375
- update_offset: float32 [2, 256], replicated, may hold values from -3 to 3
Outputs:
- embedding: bfloat16 [393216, 256], P(('wide', 'narrow'))
- input_gradient: float32 [393216, 256], P(('wide', 'narrow'))
- message_gradient: float32 [2, 256, 256], replicated
- offset_gradient: float32 [2, 256], replicated
- self_gradient: float32 [2, 256, 256], replicated
- neighbor_gradient: float32 [2, 256, 256], replicated
- update_gradient: float32 [2, 256], replicated
Inputs may be any that keep to these rules, and one draw needn't show every extreme that they name: `visit_counts`: every entry is a whole number. Row s * 1536 + r * 2 + c is zero exactly where target_rows[r, s * 2 + c] is 512, and has a positive count otherwise. `target_rows`: in every draw some device receives a live row in every one of its 1536 positions; live rows never target the last 64 local nodes.
All inputs are finite; a program needn't handle non-finite values.
Results may differ from a plain program's by a relative error of at most 0.0075.
Values may be sent and summed in bfloat16 or wider, within the bound.
A program may use at most 32 MiB of HBM per device.

v0:
```python
import jax
import jax.numpy as jnp
from jax import lax
from jax.sharding import PartitionSpec as P

CAP = 2
LAYERS = 2


epsilon = 1e-05


def silu_slope(value):
    sigma = jax.nn.sigmoid(value)
    return sigma * (1.0 + value * (1.0 - sigma))


def normalize(update_pre):
    activated = jax.nn.silu(update_pre)
    scaling = lax.rsqrt(jnp.mean(activated * activated, axis=-1, keepdims=True) + epsilon)
    return (activated, scaling)


def norm_backward(upward, update_pre):
    activated, scaling = normalize(update_pre)
    inner = jnp.mean(upward * activated, axis=-1, keepdims=True)
    slope = scaling * upward - activated * (scaling * scaling * scaling) * inner
    return slope * silu_slope(update_pre)


def left_contract(first, second):
    return lax.dot_general(
        first, second, (((0,), (0,)), ((), ())), preferred_element_type=jnp.float32
    )


def right_contract(first, second):
    return lax.dot_general(
        first, second, (((1,), (1,)), ((), ())), preferred_element_type=jnp.float32
    )


def body(
    features,
    upstream,
    visit_counts,
    target_rows,
    message_weight,
    message_offset,
    self_weight,
    neighbor_weight,
    update_offset,
):
    wide_count = lax.axis_size("wide")
    narrow_count = lax.axis_size("narrow")
    local_rows = features.shape[0]
    width = features.shape[1]
    slot_count = visit_counts.shape[0]
    totals = jnp.sum(visit_counts, axis=1, dtype=jnp.float32).astype(jnp.bfloat16)
    targets = target_rows[0]
    matches = targets[None, :] == jnp.arange(local_rows, dtype=jnp.int32)[:, None]
    selector = matches.astype(jnp.bfloat16)
    states = features
    saved = []
    for layer in range(LAYERS):
        message_pre = (
            jnp.dot(states, message_weight[layer], preferred_element_type=jnp.float32)
            + message_offset[layer]
        )
        messages = jax.nn.silu(message_pre).astype(jnp.bfloat16)
        partial_rows = jnp.dot(visit_counts, messages, preferred_element_type=jnp.float32).astype(
            jnp.bfloat16
        )
        forward_shaped = partial_rows.reshape(wide_count, narrow_count, CAP, width)
        totals_grid = totals.reshape(wide_count, narrow_count, CAP)
        arrived = lax.all_to_all(
            lax.all_to_all(forward_shaped, "wide", split_axis=0, concat_axis=0, tiled=True),
            "narrow",
            split_axis=1,
            concat_axis=1,
            tiled=True,
        )
        arrived_totals = lax.all_to_all(
            lax.all_to_all(totals_grid, "wide", split_axis=0, concat_axis=0, tiled=True),
            "narrow",
            split_axis=1,
            concat_axis=1,
            tiled=True,
        )
        arrived, arrived_totals = (
            arrived.reshape(slot_count, width),
            arrived_totals.reshape(slot_count),
        )
        weight_sum = jnp.sum(
            jnp.where(matches, arrived_totals.astype(jnp.float32)[None, :], 0.0), axis=1
        )
        divisor = jnp.maximum(weight_sum, 1.0)[:, None]
        gathered = jnp.dot(selector, arrived, preferred_element_type=jnp.float32)
        neighbor_mean = (gathered / divisor).astype(jnp.bfloat16)
        update_pre = (
            jnp.dot(states, self_weight[layer], preferred_element_type=jnp.float32)
            + jnp.dot(neighbor_mean, neighbor_weight[layer], preferred_element_type=jnp.float32)
            + update_offset[layer]
        )
        activated, scaling = normalize(update_pre)
        saved.append((states, message_pre, neighbor_mean, update_pre, divisor))
        states = (activated * scaling).astype(jnp.bfloat16)
    upward = upstream.astype(jnp.float32)
    grads = [None] * LAYERS
    for layer in reversed(range(LAYERS)):
        states_in, message_pre, neighbor_mean, update_pre, divisor = saved[layer]
        slope = norm_backward(upward, update_pre)
        slope_b = slope.astype(jnp.bfloat16)
        mean_slope = right_contract(slope_b, neighbor_weight[layer])
        spread = (mean_slope / divisor).astype(jnp.bfloat16)
        padded = jnp.concatenate([spread, jnp.zeros((1, width), jnp.bfloat16)], axis=0)
        shaped = padded[targets].reshape(wide_count, narrow_count, CAP, width)
        returned = lax.all_to_all(
            lax.all_to_all(shaped, "wide", split_axis=0, concat_axis=0, tiled=True),
            "narrow",
            split_axis=1,
            concat_axis=1,
            tiled=True,
        )
        returned = returned.reshape(slot_count, width)
        self_grad = left_contract(states_in, slope_b)
        neighbor_grad = left_contract(neighbor_mean, slope_b)
        update_grad = jnp.sum(slope, axis=0)
        lower = right_contract(slope_b, self_weight[layer])
        message_slope = left_contract(visit_counts, returned)
        pre_slope = message_slope * silu_slope(message_pre)
        pre_b = pre_slope.astype(jnp.bfloat16)
        message_grad = left_contract(states_in, pre_b)
        offset_grad = jnp.sum(pre_slope, axis=0)
        upward = lower + right_contract(pre_b, message_weight[layer])
        layer_terms = (message_grad, offset_grad, self_grad, neighbor_grad, update_grad)
        grads[layer] = layer_terms
    stacked = [jnp.stack([entry[position] for entry in grads]) for position in range(5)]
    stacked = lax.psum(
        (stacked[0], stacked[1], stacked[2], stacked[3], stacked[4]), ("wide", "narrow")
    )
    return (states, upward, stacked[0], stacked[1], stacked[2], stacked[3], stacked[4])


def solution(mesh):
    in_specs = (
        P(("wide", "narrow"), None),
        P(("wide", "narrow"), None),
        P(("wide", "narrow"), None),
        P(("wide", "narrow"), None),
        P(),
        P(),
        P(),
        P(),
        P(),
    )
    out_specs = (P(("wide", "narrow"), None), P(("wide", "narrow"), None), P(), P(), P(), P(), P())
    return jax.shard_map(body, mesh=mesh, in_specs=in_specs, out_specs=out_specs, check_vma=False)
```

profile of v0, /device:TPU:1, one launch (start us, length us, event | category | flops | bytes accessed | tf_op | source)
XLA Modules:
  0.0 845.0 jit_solution(3290003440669812690)
XLA Ops:
  7.2 1.8 reduce_sum.105
  9.3 1.1 copy.109
  10.4 14.5 %all-to-all-start.2 = ((bf16[64,12,2]{1,2,0:T(2,128)(2,1)}), bf16[64,12,2]{1,2,0:T(2,128)(2,1)S(1)}, u32[]{:S(2)}, u32[]{:S(2)}) async-start(bf16[64,12,2]{1,2,0:T(2,128)(2,1)} %copy.109), calls=%async_computation.2 | async-start | bytes 65536 | tf_op jit(solution)/shard_map/all_to_all | solution.py:84
  25.3 0.8 copy-done.12
  26.1 0.6 fusion.2
  27.0 1.2 reshape.118
  28.2 6.2 all-to-all-done.2
  34.4 4.7 all-to-all-start
  39.1 0.7 copy.110
  39.8 22.3 %all-to-all-done = bf16[64,12,2,256]{3,2,1,0:T(2,128)(2,1)S(1)} async-done(((bf16[64,12,2,256]{3,2,1,0:T(2,128)(2,1)}), bf16[64,12,2,256]{3,2,1,0:T(2,128)(2,1)S(1)}, u32[]{:S(2)}, u32[]{:S(2)}) %all-to-all-start) | async-done | bytes 786464 | tf_op jit(solution)/shard_map/all_to_all | solution.py:77
  62.1 11.9 %all-to-all-start.3 = ((bf16[64,12,2]{0,2,1:T(2,128)(2,1)}), bf16[64,12,2]{0,2,1:T(2,128)(2,1)S(1)}, u32[]{:S(2)}, u32[]{:S(2)}) async-start(bf16[64,12,2]{0,2,1:T(2,128)(2,1)} %copy.110), calls=%async_computation.3 | async-start | bytes 12288 | tf_op jit(solution)/shard_map/all_to_all | solution.py:83
  74.0 1.6 copy.107
  75.6 7.2 all-to-all-done.3
  82.8 3.6 all-to-all-start.1
  86.6 1.1 fusion.37
  88.1 0.4 select_reduce_fusion
  88.5 25.8 %all-to-all-done.1 = bf16[64,12,2,256]{3,2,0,1:T(2,128)(2,1)S(1)} async-done(((bf16[64,12,2,256]{3,2,0,1:T(2,128)(2,1)}), bf16[64,12,2,256]{3,2,0,1:T(2,128)(2,1)S(1)}, u32[]{:S(2)}, u32[]{:S(2)}) %all-to-all-start.1) | async-done | bytes 786464 | tf_op jit(solution)/shard_map/all_to_all | solution.py:76
  114.3 0.5 copy.108
  114.8 0.3 reshape.119
  115.2 0.6 fusion.13
  115.8 0.4 copy-done.9
  116.2 0.4 multiply_reduce_fusion.2
  116.8 0.4 copy-done.6
  117.2 1.1 convolution_add_fusion.3
  118.3 2.6 fusion.3
  120.8 1.4 copy.113
  122.2 0.3 reshape.121
  122.5 34.7 %all_to_all.52 = bf16[64,12,2,256]{3,2,1,0:T(2,128)(2,1)S(1)} all-to-all(bf16[64,12,2,256]{3,2,1,0:T(2,128)(2,1)S(1)} %reshape.121), channel_id=1, replica_groups=mesh['wide'=64,'narrow'=12] {'wide'}, dimensions={0} | all-to-all | bytes 1572864 | tf_op jit(solution)/shard_map/all_to_all | solution.py:77
  157.3 1.6 copy.114
  158.9 3.8 all-to-all-start.5
  162.9 1.1 fusion.29
  164.0 26.5 %all-to-all-done.5 = bf16[64,12,2,256]{3,2,0,1:T(2,128)(2,1)S(1)} async-done(((bf16[64,12,2,256]{3,2,0,1:T(2,128)(2,1)}), bf16[64,12,2,256]{3,2,0,1:T(2,128)(2,1)S(1)}, u32[]{:S(2)}, u32[]{:S(2)}) %all-to-all-start.5) | async-done | bytes 786464 | tf_op jit(solution)/shard_map/all_to_all | solution.py:76
  190.5 0.5 copy.115
  191.4 0.6 fusion.12
  192.1 0.4 copy-done.10
  192.5 0.4 fusion.18
  193.0 1.0 fusion.59
  194.3 4.8 gather_fusion
  199.4 34.6 %all_to_all.53 = bf16[64,12,2,256]{3,2,1,0:T(2,128)(2,1)S(1)} all-to-all(bf16[64,12,2,256]{3,2,1,0:T(2,128)(2,1)S(1)} %reshape.123), channel_id=1, replica_groups=mesh['wide'=64,'narrow'=12] {'wide'}, dimensions={0} | all-to-all | bytes 1572864 | tf_op jit(solution)/shard_map/all_to_all | solution.py:119
  234.0 1.6 copy.117
  235.6 3.6 all-to-all-start.7
  239.3 1.0 fusion.27
  240.3 27.0 %all-to-all-done.7 = bf16[64,12,2,256]{3,2,0,1:T(2,128)(2,1)S(1)} async-done(((bf16[64,12,2,256]{3,2,0,1:T(2,128)(2,1)}), bf16[64,12,2,256]{3,2,0,1:T(2,128)(2,1)S(1)}, u32[]{:S(2)}, u32[]{:S(2)}) %all-to-all-start.7) | async-done | bytes 786464 | tf_op jit(solution)/shard_map/all_to_all | solution.py:118
  267.3 0.5 copy.118
  268.1 2.3 fusion.63
  270.8 0.4 fusion.58
  271.2 0.3 copy-done.27
  271.8 4.8 gather_fusion.1
  276.9 34.7 %all_to_all.54 = bf16[64,12,2,256]{3,2,1,0:T(2,128)(2,1)S(1)} all-to-all(bf16[64,12,2,256]{3,2,1,0:T(2,128)(2,1)S(1)} %reshape.125), channel_id=1, replica_groups=mesh['wide'=64,'narrow'=12] {'wide'}, dimensions={0} | all-to-all | bytes 1572864 | tf_op jit(solution)/shard_map/all_to_all | solution.py:119
  311.6 1.6 copy.121
  313.2 3.8 all-to-all-start.9
  318.1 0.8 pad_maximum_fusion.2
  319.1 0.8 pad_maximum_fusion.1
  320.2 24.7 %all-to-all-done.9 = bf16[64,12,2,256]{3,2,0,1:T(2,128)(2,1)S(1)} async-done(((bf16[64,12,2,256]{3,2,0,1:T(2,128)(2,1)}), bf16[64,12,2,256]{3,2,0,1:T(2,128)(2,1)S(1)}, u32[]{:S(2)}, u32[]{:S(2)}) %all-to-all-start.9) | async-done | bytes 786464 | tf_op jit(solution)/shard_map/all_to_all | solution.py:118
  345.0 0.5 copy.122
  345.8 2.1 fusion.64
  348.2 0.8 pad_maximum_fusion
  349.1 0.8 copy.125
  350.2 110.7 %all-reduce.2 = (f32[2,256]{1,0:T(2,128)}, f32[2,256]{1,0:T(2,128)}) all-reduce(f32[2,256]{1,0:T(2,128)S(1)} %pad_maximum_fusion.3, f32[2,256]{1,0:T(2,128)S(1)} %pad_maximum_fusion.4), channel_id=1, replica_groups=mesh['wide'=64,'narrow'=12] {'wide','narrow'}, use_global_device_ids=true, to_apply=%region_9.10 | all-reduce | flops 1024 | bytes 8192 | tf_op jit(solution)/shard_map/psum | solution.py:139
  460.9 1.1 convolution_add_fusion.1
  461.9 371.3 %all-reduce.6.cloned.1.call-done = (f32[2,256,256]{1,2,0:T(8,128)}, f32[2,256,256]{1,2,0:T(8,128)}, f32[2,256,256]{2,1,0:T(8,128)}) async-done(((f32[2,256,256]{1,2,0:T(8,128)}, f32[2,256,256]{1,2,0:T(8,128)}, f32[2,256,256]{2,1,0:T(8,128)}), (f32[2,256,256]{1,2,0:T(8,128)}, f32[2,256,256]{1,2,0:T(8,128)}, f32[2,256,256]{2,1,0:T(8,128)})) %all-reduce.6.cloned.1.call-update) | async-done | bytes 1572880 | tf_op jit(solution)/shard_map/psum | solution.py:139
  833.2 2.1 copy.126
  835.3 2.0 copy.127
  837.4 0.8 copy.137
  (88 shorter events, 6.3 us)
Async XLA Ops:
  7.2 17.8 %copy-start = (bf16[512,256]{1,0:T(8,128)(2,1)S(1)}, bf16[512,256]{1,0:T(8,128)(2,1)}, u32[]{:S(2)}) copy-start(bf16[512,256]{1,0:T(8,128)(2,1)} %param.9) | copy-start | bytes 786436
  7.2 18.9 %copy-start.1 = (bf16[1536,512]{1,0:T(8,128)(2,1)S(1)}, bf16[1536,512]{1,0:T(8,128)(2,1)}, u32[]{:S(2)}) copy-start(bf16[1536,512]{1,0:T(8,128)(2,1)} %param.11) | copy-start | bytes 4718596
  7.2 17.8 %copy-start.23 = (f32[2,256]{1,0:T(2,128)S(1)}, f32[2,256]{1,0:T(2,128)}, u32[]{:S(2)}) copy-start(f32[2,256]{1,0:T(2,128)} %param.14) | copy-start | bytes 6148
  7.2 17.8 %copy-start.5 = (bf16[2,256,256]{2,1,0:T(8,128)(2,1)S(1)}, bf16[2,256,256]{2,1,0:T(8,128)(2,1)}, u32[]{:S(2)}) copy-start(bf16[2,256,256]{2,1,0:T(8,128)(2,1)} %param.13) | copy-start | bytes 786436
  10.4 24.0 %all-to-all-start.2 = ((bf16[64,12,2]{1,2,0:T(2,128)(2,1)}), bf16[64,12,2]{1,2,0:T(2,128)(2,1)S(1)}, u32[]{:S(2)}, u32[]{:S(2)}) async-start(bf16[64,12,2]{1,2,0:T(2,128)(2,1)} %copy.109), calls=%async_computation.2 | async-start | bytes 65536 | tf_op jit(solution)/shard_map/all_to_all | solution.py:84
  25.3 0.8 copy-start.12
  34.4 27.8 %all-to-all-start = ((bf16[64,12,2,256]{3,2,1,0:T(2,128)(2,1)}), bf16[64,12,2,256]{3,2,1,0:T(2,128)(2,1)S(1)}, u32[]{:S(2)}, u32[]{:S(2)}) async-start(bf16[64,12,2,256]{3,2,1,0:T(2,128)(2,1)} %reshape.118), calls=%async_computation | async-start | bytes 1572864 | tf_op jit(solution)/shard_map/all_to_all | solution.py:77
  62.1 20.7 %all-to-all-start.3 = ((bf16[64,12,2]{0,2,1:T(2,128)(2,1)}), bf16[64,12,2]{0,2,1:T(2,128)(2,1)S(1)}, u32[]{:S(2)}, u32[]{:S(2)}) async-start(bf16[64,12,2]{0,2,1:T(2,128)(2,1)} %copy.110), calls=%async_computation.3 | async-start | bytes 12288 | tf_op jit(solution)/shard_map/all_to_all | solution.py:83
  74.0 12.5 %copy-start.22 = (s32[1,1536]{1,0:T(1,128)S(1)}, s32[1,1536]{1,0:T(1,128)}, u32[]{:S(2)}) copy-start(s32[1,1536]{1,0:T(1,128)} %param.12) | copy-start | bytes 18436
  74.0 12.5 %copy-start.24 = (f32[2,256]{1,0:T(2,128)S(1)}, f32[2,256]{1,0:T(2,128)}, u32[]{:S(2)}) copy-start(f32[2,256]{1,0:T(2,128)} %param.17) | copy-start | bytes 6148
  74.0 12.5 %copy-start.2 = (bf16[2,256,256]{2,1,0:T(8,128)(2,1)S(1)}, bf16[2,256,256]{2,1,0:T(8,128)(2,1)}, u32[]{:S(2)}) copy-start(bf16[2,256,256]{2,1,0:T(8,128)(2,1)} %param.15) | copy-start | bytes 786436
  82.8 31.4 %all-to-all-start.1 = ((bf16[64,12,2,256]{3,2,0,1:T(2,128)(2,1)}), bf16[64,12,2,256]{3,2,0,1:T(2,128)(2,1)S(1)}, u32[]{:S(2)}, u32[]{:S(2)}) async-start(bf16[64,12,2,256]{3,2,0,1:T(2,128)(2,1)} %copy.107), calls=%async_computation.1 | async-start | bytes 1572864 | tf_op jit(solution)/shard_map/all_to_all | solution.py:76
  115.1 1.0 copy-start.9
  115.1 1.1 copy-start.25
  115.8 1.0 copy-start.15
  116.2 0.9 copy-start.6
  157.3 5.5 copy-start.21
  157.3 5.7 copy-start.3
  158.9 31.7 %all-to-all-start.5 = ((bf16[64,12,2,256]{3,2,0,1:T(2,128)(2,1)}), bf16[64,12,2,256]{3,2,0,1:T(2,128)(2,1)S(1)}, u32[]{:S(2)}, u32[]{:S(2)}) async-start(bf16[64,12,2,256]{3,2,0,1:T(2,128)(2,1)} %copy.114), calls=%async_computation.5 | async-start | bytes 1572864 | tf_op jit(solution)/shard_map/all_to_all | solution.py:76
  191.4 1.0 copy-start.10
  191.4 1.1 copy-start.26
  192.1 0.9 copy-start.17
  235.6 31.6 %all-to-all-start.7 = ((bf16[64,12,2,256]{3,2,0,1:T(2,128)(2,1)}), bf16[64,12,2,256]{3,2,0,1:T(2,128)(2,1)S(1)}, u32[]{:S(2)}, u32[]{:S(2)}) async-start(bf16[64,12,2,256]{3,2,0,1:T(2,128)(2,1)} %copy.117), calls=%async_computation.7 | async-start | bytes 1572864 | tf_op jit(solution)/shard_map/all_to_all | solution.py:118
  268.1 2.3 copy-start.7
  268.1 2.3 copy-start.11
  270.5 0.7 copy-start.19
  270.5 1.0 copy-start.27
  311.6 5.7 copy-start.18
  313.2 4.6 copy-start.16
  313.2 31.8 %all-to-all-start.9 = ((bf16[64,12,2,256]{3,2,0,1:T(2,128)(2,1)}), bf16[64,12,2,256]{3,2,0,1:T(2,128)(2,1)S(1)}, u32[]{:S(2)}, u32[]{:S(2)}) async-start(bf16[64,12,2,256]{3,2,0,1:T(2,128)(2,1)} %copy.121), calls=%async_computation.9 | async-start | bytes 1572864 | tf_op jit(solution)/shard_map/all_to_all | solution.py:118
  317.0 516.3 %all-reduce.6.cloned.1.call-start = ((), (), s32[]{:S(2)}) async-start(), calls=%async_computation.10 | async-start | bytes 3145728 | tf_op jit(solution)/shard_map/psum | solution.py:139
  318.1 1.9 copy-start.20
  320.2 25.6 %copy-start.13 = (f32[512,256]{0,1:T(8,128)S(1)}, f32[512,256]{0,1:T(8,128)}, u32[]{:S(2)}) copy-start(f32[512,256]{0,1:T(8,128)} %copy-done.12) | copy-start | bytes 1572868
  347.9 1.1 copy-start.4
  349.0 111.8 %copy-start.8 = (bf16[2,256,256]{2,1,0:T(8,128)(2,1)S(1)}, bf16[2,256,256]{2,1,0:T(8,128)(2,1)}, u32[]{:S(2)}) copy-start(bf16[2,256,256]{2,1,0:T(8,128)(2,1)} %param.13) | copy-start | bytes 786436
  833.2 4.1 copy-start.14
Sparse Core Ops, SparseCore 0:
  349.2 484.0 all-reduce.5
where the time goes:
time: 846 us; the launch traced here: 845 us
  waiting for transfers between devices  511 us (60%)
  blocking collectives  215 us (25%)
  starting transfers between devices  46.3 us (5%)
  local copies, waits for them, and re-layouts  34.1 us (4%)
  matrix products  17.8 us (2%)
  between operations  14.7 us (2%)
    psum x1, waiting for transfers between devices, body(): lax.psum((stacked[0], stacked[1], stacked[2], stacked[3], stacked[4]), ('...  371 us
    psum x1, blocking collectives, body(): lax.psum((stacked[0], stacked[1], stacked[2], stacked[3], stacked[4]), ('...  111 us
    all_to_all x2, blocking collectives, body(): lax.all_to_all(shaped, 'wide', split_axis=0, concat_axis=0, tiled=True)  69.3 us
    all_to_all x2, waiting for transfers between devices, body(): lax.all_to_all(lax.all_to_all(forward_shaped, 'wide', split_axis=0, conca...  52.3 us
    all_to_all x2, waiting for transfers between devices, body(): lax.all_to_all(lax.all_to_all(shaped, 'wide', split_axis=0, concat_axis=0...  51.7 us
    all_to_all x1, blocking collectives, body(): lax.all_to_all(forward_shaped, 'wide', split_axis=0, concat_axis=0, tiled...  34.7 us
    all_to_all x1, waiting for transfers between devices, body(): lax.all_to_all(forward_shaped, 'wide', split_axis=0, concat_axis=0, tiled...  22.3 us
  transfers between devices with their start and end apart: 8, of which 8 were waited for; matrix products, arithmetic and copies ran while one was open for 2% of the time, Pallas kernels for 0%

commit v1 on v0

v1 whole, which is shorter than its diff:
```python
import functools

import jax
import jax.numpy as jnp
from jax import lax
from jax.experimental import pallas as pl
from jax.experimental.pallas import tpu as pltpu
from jax.sharding import PartitionSpec as P

F = 256
H = 128
NX = 4
NC = 2
GROUP = NX * NC
EPS = 1e-05
BF = jnp.bfloat16
F32 = jnp.float32
MESH = pl.DeviceIdType.MESH


def sigmoid(v):
    return 1.0 / (1.0 + jnp.exp(-v))


def silu_slope(v):
    sigma = sigmoid(v)
    return sigma * (1.0 + v * (1.0 - sigma))


def dot(a, b):
    return jnp.dot(a, b, preferred_element_type=F32)


def dot_nt(a, b):
    return lax.dot_general(a, b, (((1,), (1,)), ((), ())), preferred_element_type=F32)


def dot_tn(a, b):
    return lax.dot_general(a, b, (((0,), (0,)), ((), ())), preferred_element_type=F32)


def iota(shape, dim):
    return lax.broadcasted_iota(jnp.int32, shape, dim)


def pair_permutation(blocks):
    n = 16 * blocks
    out = iota((n, n), 0)
    source = ((out // 2) % 8) * (2 * blocks) + (out // 16) * 2 + out % 2
    return jnp.where(iota((n, n), 1) == source, 1.0, 0.0).astype(BF)


def alternate(t, n):
    s = (t + 1) // 2
    return lax.rem(s + (1 - lax.rem(t, 2)) * (n - 2 * s), n)


def kernel(
    NW, NZ, R,
    feat, ups, cnt, t_n, t_t, t_y, wm, bm, ws, wn, bu,
    emb, ing, gm, go, gs, gn, gu,
    ct, cnt_n, cnt_t, sel_n, sel_t, selt_n, selt_t, m1, m2,
    pre, upre, st, nm, base, low, div,
    sa, za, ma, xa, sb, xb, mb, zb,
    xs, xr, ys, yr,
    g1s, g1r, g1a, g1b, g1c, g1d, g1e, g1f, g1g,
    g2s, g2r, g2a, g2b, g2c, g2d, g2e, g2f, g2g,
    ssem, rsem,
):
    NP = NW // NC
    NY = NP // NX
    B = NC * NZ
    PR, BR = 2 * B, 2 * NP
    S = NP * PR
    wide = lax.axis_index("wide")
    z = lax.axis_index("narrow")
    p, c = wide // NC, lax.rem(wide, NC)
    y, x = p // NX, lax.rem(p, NX)
    q = lax.rem(wide, GROUP)
    b = c * NZ + z

    def plane_peer(d):
        dy = alternate(d // NX, NY)
        yy, xx = lax.rem(y + dy, NY), lax.rem(x + lax.rem(d, NX), NX)
        pp = yy * NX + xx
        return pp, (pp * NC + c, z)

    def column_peer(j):
        dz = alternate(j // 2, NZ)
        cc, zz = lax.rem(c + lax.rem(j, 2), NC), lax.rem(z + dz, NZ)
        return cc * NZ + zz, (p * NC + cc, zz)

    def group_peer(j):
        qq = lax.rem(q + j, GROUP)
        return qq, (y * GROUP + qq, z)

    def row_peer(j):
        yy = lax.rem(y + j, NY)
        return yy, (yy * GROUP + q, z)

    def ring_peer(j):
        zz = lax.rem(z + j, NZ)
        return zz, (wide, zz)

    def send(src, dst, slot, target):
        pltpu.make_async_remote_copy(
            src_ref=src, dst_ref=dst, send_sem=ssem.at[slot], recv_sem=rsem.at[slot],
            device_id=target, device_id_type=MESH,
        ).start()

    def scatter(src, dst, slot, mine, peer, n):
        def step(i, _):
            theirs, target = peer(n - i)
            send(src.at[theirs], dst.at[mine], slot, target)
            return _
        lax.fori_loop(1, n, step, 0)
        dst[pl.ds(mine, 1)] = src[pl.ds(mine, 1)]

    def spread_out(src, dst, slot, mine, peer, n):
        def step(i, _):
            send(src, dst.at[mine], slot, peer(n - i)[1])
            return _
        lax.fori_loop(1, n, step, 0)
        dst[pl.ds(mine, 1)] = src[...][None]

    def await_bytes(ref, sem):
        pltpu.make_async_copy(ref, ref, sem).wait()

    def arrived(dst, slot):
        await_bytes(dst.at[pl.ds(0, dst.shape[0] - 1)], rsem.at[slot])

    barrier = pltpu.get_barrier_semaphore()

    def greet(peer, first, last):
        def step(i, _):
            pl.semaphore_signal(barrier, inc=1, device_id=peer(i)[1], device_id_type=MESH)
            return _
        lax.fori_loop(first, last, step, 0)

    greet(plane_peer, 1, NP)
    greet(column_peer, 1, B)
    greet(lambda i: (i, ((y * NX + lax.rem(x + i, NX)) * NC + (1 - c), z)), 1, NX)

    def to_t_order(src, dst, width):
        for o in range(NP // 8):
            got = dot(m1[...], src[o * 8 * PR:(o + 1) * 8 * PR, :]).astype(BF)
            got = got.reshape(B, 16, width)
            for i in range(B):
                dst[i * BR + o * 16:i * BR + (o + 1) * 16, :] = got[i]

    def shuffle_b(i):
        for o in range(NP // 8):
            got = dot(m1[...], xb[i, o * 8:(o + 1) * 8].reshape(8 * PR, H)).astype(BF)
            mb[i, :, o * 16:(o + 1) * 16, :] = got.reshape(B, 16, H)

    def shuffle_a(i):
        for o in range(B // 8):
            got = dot(m2[...], za[i, o * 8:(o + 1) * 8].reshape(8 * BR, H)).astype(BF)
            ma[i, :, o * 16:(o + 1) * 16, :] = got.reshape(NP, 16, H)

    def fill_a(i, left, right):
        n = max(1, B // 6)
        rows = S // n
        for k in range(n):
            got = dot(left[k * rows:(k + 1) * rows, :], right).astype(BF)
            sa[i, k * (B // n):(k + 1) * (B // n)] = got.reshape(B // n, BR, H)

    def fill_b(i, left, right):
        n = NP // 8
        rows = S // n
        for k in range(n):
            got = dot(left[k * rows:(k + 1) * rows, :], right).astype(BF)
            sb[i, k * 8:(k + 1) * 8] = got.reshape(8, PR, H)

    def first_a(i):
        scatter(sa.at[i], za.at[i], 4 * i, b, column_peer, B)

    def first_b(i):
        scatter(sb.at[i], xb.at[i], 4 * i + 1, p, plane_peer, NP)

    def second_b(i):
        arrived(xb.at[i], 4 * i + 1)
        shuffle_b(i)
        scatter(mb.at[i], zb.at[i], 4 * i + 2, b, column_peer, B)

    def second_a(i):
        arrived(za.at[i], 4 * i)
        shuffle_a(i)
        scatter(ma.at[i], xa.at[i], 4 * i + 3, p, plane_peer, NP)

    def final_a(i):
        arrived(xa.at[i], 4 * i + 3)
        return xa[i].reshape(S, H)

    def final_b(i):
        arrived(zb.at[i], 4 * i + 2)
        return zb[i].reshape(S, H)

    def place(buf, matrix, value):
        g = value.astype(BF)
        for k in range(GROUP):
            for h in range(2):
                buf[k, matrix * 64 + h * 32:matrix * 64 + (h + 1) * 32, :] = (
                    g[k * 32:(k + 1) * 32, h * H:(h + 1) * H])

    def place_vectors(buf, rows, vectors):
        tile = jnp.zeros((16, H), F32)
        line = iota((16, H), 0)
        for v, vec in enumerate(vectors):
            for h in range(2):
                tile = jnp.where(line == 2 * v + h, vec[:, h * H:(h + 1) * H], tile)
        for k in range(GROUP):
            buf[k, rows:rows + 16, :] = tile.astype(BF)

    def reduce_1(bufs, slot):
        scatter(bufs[0], bufs[1], slot, q, group_peer, GROUP)

    def reduce_2(bufs, slot):
        s, r, a = bufs[:3]
        arrived(r, slot)
        rows = s.shape[1] - 16
        piece = rows // NY
        total = r[0].astype(F32)
        for k in range(1, GROUP):
            total = total + r[k].astype(F32)
        for k in range(NY):
            a[k, 0:piece, :] = total[k * piece:(k + 1) * piece]
            a[k, piece:piece + 8, :] = total[rows:rows + 8]
        scatter(a, bufs[3], slot + 1, y, row_peer, NY)

    def reduce_3(bufs, slot):
        r, s = bufs[3], bufs[4]
        arrived(r, slot + 1)
        total = r[0]
        for k in range(1, NY):
            total = total + r[k]
        s[...] = total
        spread_out(s, bufs[5], slot + 2, z, ring_peer, NZ)

    def reduce_4(bufs, slot):
        r, s = bufs[5], bufs[6]
        arrived(r, slot + 2)
        total = r[0]
        for k in range(1, NZ):
            total = total + r[k]
        s[...] = total
        piece = s.shape[0] - 8
        src, dst = s.at[pl.ds(0, piece)], bufs[7]

        def step(i, _):
            send(src, dst.at[y], slot + 3, row_peer(NY - i)[1])
            return _
        lax.fori_loop(1, NY, step, 0)
        dst[pl.ds(y, 1)] = s[0:piece][None]

    def reduce_5(bufs, slot):
        r, out = bufs[7], bufs[8]
        arrived(r, slot + 3)
        rows = out.shape[1]
        out[pl.ds(q, 1)] = r[...].reshape(1, rows, H).astype(BF)

        def step(i, _):
            send(out.at[q], out.at[q], slot + 4, group_peer(GROUP - i)[1])
            return _
        lax.fori_loop(1, GROUP, step, 0)

    def take(bufs, matrix, write):
        out = bufs[8]
        for k in range(GROUP):
            for h in range(2):
                got = out[k, matrix * 64 + h * 32:matrix * 64 + (h + 1) * 32, :].astype(F32)
                write(slice(k * 32, (k + 1) * 32), slice(h * H, (h + 1) * H), got)

    def take_vector(bufs, index, ref, layer):
        s = bufs[6]
        rows = s.shape[0] - 8
        for h in range(2):
            ref[layer:layer + 1, h * H:(h + 1) * H] = (
                s[rows + 2 * index + h:rows + 2 * index + h + 1, :])

    bufs1 = (g1s, g1r, g1a, g1b, g1c, g1d, g1e, g1f, g1g)
    bufs2 = (g2s, g2r, g2a, g2b, g2c, g2d, g2e, g2f, g2g)
    TOT, RED1, RED2 = 16, 18, 23

    def message_half(layer, states):
        value = dot(states, wm[layer]) + bm[layer:layer + 1, :]
        pre[layer] = value
        return (value * sigmoid(value)).astype(BF)

    m1[...] = pair_permutation(B)
    to_t_order(cnt, ct, R)
    states = feat[...]
    st[0] = states
    for layer in range(2):
        messages = message_half(layer, st[layer])
        fill_a(layer, ct, messages[:, :H])
        if layer == 0:
            pl.semaphore_wait(barrier, NP - 1 + B - 1 + NX - 1)
        first_a(layer)
        fill_b(layer, cnt, messages[:, H:])
        first_b(layer)
        if layer == 0:
            totals = jnp.sum(cnt[...].astype(F32), axis=1, keepdims=True).astype(BF)
            line = lax.rem(iota((S, H), 0), PR)
            spreaded = jnp.where(line == iota((S, H), 1), totals.astype(F32), 0.0).astype(BF)
            pick = jnp.where(iota((NP, S), 1) // PR == iota((NP, S), 0), 1.0, 0.0).astype(BF)
            xs[...] = dot(pick, spreaded).reshape(NP, 1, H)
            scatter(xs, xr, TOT, p, plane_peer, NP)
            m2[...] = pair_permutation(NP)
            sel_n[...] = jnp.where(iota((R, S), 0) == t_n[...], 1.0, 0.0).astype(BF)
        base[...] = dot(st[layer], ws[layer]) + bu[layer:layer + 1, :]
        second_b(layer)
        second_a(layer)
        if layer == 0:
            arrived(xr, TOT)
            grid = xr[...].reshape(NP, H).astype(BF)
            lane = iota((B, H), 1)
            turned = jnp.zeros((B, H), F32)
            for k in range(2):
                chosen = jnp.where(lane == 2 * iota((B, H), 0) + k, 1.0, 0.0).astype(BF)
                put = jnp.where(iota((NP, H), 1) == 2 * iota((NP, H), 0) + k, 1.0, 0.0).astype(BF)
                turned = turned + dot(dot_nt(chosen, grid).astype(BF), put)
            ys[...] = turned.reshape(B, 1, H)
            scatter(ys, yr, TOT + 1, b, column_peer, B)
            sel_t[...] = jnp.where(iota((R, S), 0) == t_t[...], 1.0, 0.0).astype(BF)
            selt_n[...] = sel_n[...].T
            selt_t[...] = sel_t[...].T
            arrived(yr, TOT + 1)

            def add(k, total):
                hit = iota((R, H), 0) == t_y[k]
                return total + jnp.where(hit, yr[k], 0.0)
            weight = lax.fori_loop(0, B, add, jnp.zeros((R, H), F32))
            div[...] = jnp.maximum(jnp.sum(weight, axis=1, keepdims=True), 1.0)
        else:
            cnt_n[...] = cnt[...].T
            cnt_t[...] = ct[...].T
        divisor = div[...]
        nm[layer, :, H:] = (dot(sel_t[...], final_b(layer)) / divisor).astype(BF)
        nm[layer, :, :H] = (dot(sel_n[...], final_a(layer)) / divisor).astype(BF)
        value = base[...] + dot(nm[layer], wn[layer])
        upre[layer] = value
        activated = value * sigmoid(value)
        scaling = lax.rsqrt(jnp.mean(activated * activated, axis=-1, keepdims=True) + EPS)
        states = (activated * scaling).astype(BF)
        if layer == 0:
            st[1] = states
        else:
            emb[...] = states

    for turn, layer in ((2, 1), (3, 0)):
        upward = ups[...].astype(F32) if layer == 1 else low[...]
        value = upre[layer]
        activated = value * sigmoid(value)
        scaling = lax.rsqrt(jnp.mean(activated * activated, axis=-1, keepdims=True) + EPS)
        inner = jnp.mean(upward * activated, axis=-1, keepdims=True)
        slope = scaling * upward - activated * (scaling * scaling * scaling) * inner
        slope = slope * silu_slope(value)
        slope_b = slope.astype(BF)
        spread = (dot_nt(slope_b, wn[layer]) / div[...]).astype(BF)
        fill_a(turn, selt_t, spread[:, :H])
        first_a(turn)
        fill_b(turn, selt_n, spread[:, H:])
        first_b(turn)
        update_grad = jnp.sum(slope, axis=0, keepdims=True)
        place(g1s, 0 if layer == 1 else 3, dot_tn(st[layer], slope_b))
        place(g1s, 1 if layer == 1 else 4, dot_tn(nm[layer], slope_b))
        low[...] = dot_nt(slope_b, ws[layer])
        if layer == 1:
            first_update = update_grad
        else:
            place_vectors(g1s, 320, (first_update, first_offset, update_grad))
            reduce_1(bufs1, RED1)
        second_b(turn)
        second_a(turn)
        if layer == 0:
            reduce_2(bufs1, RED1)
            reduce_3(bufs1, RED1)
            reduce_4(bufs1, RED1)
            reduce_5(bufs1, RED1)
        slope_left = dot(cnt_n[...], final_a(turn))
        slope_right = dot(cnt_t[...], final_b(turn))
        pre_slope = jnp.concatenate([slope_left, slope_right], axis=1) * silu_slope(pre[layer])
        pre_b = pre_slope.astype(BF)
        offset_grad = jnp.sum(pre_slope, axis=0, keepdims=True)
        if layer == 1:
            place(g1s, 2, dot_tn(st[1], pre_b))
            first_offset = offset_grad
            low[...] = low[...] + dot_nt(pre_b, wm[1])
        else:
            place(g2s, 0, dot_tn(st[0], pre_b))
            place_vectors(g2s, 64, (offset_grad,))
            reduce_1(bufs2, RED2)
            ing[...] = low[...] + dot_nt(pre_b, wm[0])
    reduce_2(bufs2, RED2)
    reduce_3(bufs2, RED2)

    await_bytes(g1g.at[pl.ds(0, GROUP - 1)], rsem.at[RED1 + 4])
    for matrix, ref, layer in ((0, gs, 1), (1, gn, 1), (2, gm, 1), (3, gs, 0), (4, gn, 0)):
        def write(rows, columns, got, ref=ref, layer=layer):
            ref[layer, rows, columns] = got
        take(bufs1, matrix, write)
    take_vector(bufs1, 0, gu, 1)
    take_vector(bufs1, 1, go, 1)
    take_vector(bufs1, 2, gu, 0)

    reduce_4(bufs2, RED2)
    reduce_5(bufs2, RED2)
    await_bytes(g2g.at[pl.ds(0, GROUP - 1)], rsem.at[RED2 + 4])

    def write_last(rows, columns, got):
        gm[0, rows, columns] = got
    take(bufs2, 0, write_last)
    take_vector(bufs2, 0, go, 0)

    for i in range(4):
        await_bytes(sa.at[i, pl.ds(0, B - 1)], ssem.at[4 * i])
        await_bytes(sb.at[i, pl.ds(0, NP - 1)], ssem.at[4 * i + 1])
        await_bytes(mb.at[i, pl.ds(0, B - 1)], ssem.at[4 * i + 2])
        await_bytes(ma.at[i, pl.ds(0, NP - 1)], ssem.at[4 * i + 3])
    await_bytes(xs.at[pl.ds(0, NP - 1)], ssem.at[TOT])
    await_bytes(ys.at[pl.ds(0, B - 1)], ssem.at[TOT + 1])
    for bufs, slot in ((bufs1, RED1), (bufs2, RED2)):
        await_bytes(bufs[1].at[pl.ds(0, GROUP - 1)], ssem.at[slot])
        await_bytes(bufs[3].at[pl.ds(0, NY - 1)], ssem.at[slot + 1])
        await_bytes(bufs[5].at[pl.ds(0, NZ - 1)], ssem.at[slot + 2])
        await_bytes(bufs[7].at[pl.ds(0, NY - 1)], ssem.at[slot + 3])
        await_bytes(bufs[8].at[pl.ds(0, GROUP - 1)], ssem.at[slot + 4])


def body(NW, NZ, features, upstream, visit_counts, target_rows, wm, bm, ws, wn, bu):
    R = features.shape[0]
    S = visit_counts.shape[0]
    NP, B, NY = NW // NC, NC * NZ, NW // GROUP
    turned = target_rows[0].reshape(NP, B, 2).transpose(1, 0, 2)
    t_t = turned.reshape(1, S)
    t_y = jnp.pad(turned.reshape(B, 1, 2 * NP), ((0, 0), (0, 0), (0, H - 2 * NP)), constant_values=R)

    def sum_buffers(matrices):
        rows = 64 * matrices
        piece = rows // NY
        return [
            pltpu.VMEM((GROUP, rows + 16, H), BF),
            pltpu.VMEM((GROUP, rows + 16, H), BF),
            pltpu.VMEM((NY, piece + 8, H), F32),
            pltpu.VMEM((NY, piece + 8, H), F32),
            pltpu.VMEM((piece + 8, H), F32),
            pltpu.VMEM((NZ, piece + 8, H), F32),
            pltpu.VMEM((piece + 8, H), F32),
            pltpu.VMEM((NY, piece, H), F32),
            pltpu.VMEM((GROUP, rows, H), BF),
        ]

    column = pltpu.VMEM((4, B, 2 * NP, H), BF)
    plane = pltpu.VMEM((4, NP, 2 * B, H), BF)
    scratch = [
        pltpu.VMEM((S, R), BF), pltpu.VMEM((R, S), BF), pltpu.VMEM((R, S), BF),
        pltpu.VMEM((R, S), BF), pltpu.VMEM((R, S), BF),
        pltpu.VMEM((S, R), BF), pltpu.VMEM((S, R), BF),
        pltpu.VMEM((16 * B, 16 * B), BF), pltpu.VMEM((16 * NP, 16 * NP), BF),
        pltpu.VMEM((2, R, F), F32), pltpu.VMEM((2, R, F), F32),
        pltpu.VMEM((2, R, F), BF), pltpu.VMEM((2, R, F), BF),
        pltpu.VMEM((R, F), F32), pltpu.VMEM((R, F), F32), pltpu.VMEM((R, 1), F32),
        column, column, plane, plane, plane, plane, column, column,
        pltpu.VMEM((NP, 1, H), F32), pltpu.VMEM((NP, 1, H), F32),
        pltpu.VMEM((B, 1, H), F32), pltpu.VMEM((B, 1, H), F32),
    ] + sum_buffers(5) + sum_buffers(1) + [
        pltpu.SemaphoreType.DMA((28,)), pltpu.SemaphoreType.DMA((28,)),
    ]
    vmem = pl.BlockSpec(memory_space=pltpu.VMEM)
    square = jax.ShapeDtypeStruct((2, F, F), F32)
    line = jax.ShapeDtypeStruct((2, F), F32)
    return pl.pallas_call(
        functools.partial(kernel, NW, NZ, R),
        out_shape=(
            jax.ShapeDtypeStruct((R, F), BF), jax.ShapeDtypeStruct((R, F), F32),
            square, line, square, square, line,
        ),
        in_specs=[vmem] * 11,
        out_specs=[vmem] * 7,
        scratch_shapes=scratch,
        compiler_params=pltpu.CompilerParams(
            collective_id=0, has_side_effects=True, vmem_limit_bytes=58 * 2**20),
        cost_estimate=pl.CostEstimate(flops=12 * 2**30, bytes_accessed=2**23, transcendentals=2**20),
    )(features, upstream, visit_counts, target_rows, t_t, t_y, wm, bm, ws, wn, bu)


def solution(mesh):
    split = P(("wide", "narrow"), None)
    in_specs = (split, split, split, split, P(), P(), P(), P(), P())
    out_specs = (split, split, P(), P(), P(), P(), P())
    run = functools.partial(body, mesh.shape["wide"], mesh.shape["narrow"])
    return jax.shard_map(run, mesh=mesh, in_specs=in_specs, out_specs=out_specs, check_vma=False)
```

time: 846 us -> 215 us (0.25)
  waiting for transfers between devices: 511 us -> 0 us
  blocking collectives: 215 us -> 0 us
  Pallas kernels: 0 us -> 204 us
  starting transfers between devices: 46.3 us -> 0 us
  local copies, waits for them, and re-layouts: 34.1 us -> 9.44 us
  matrix products: 17.8 us -> 0 us
  between operations: 14.7 us -> 0.69 us
    psum x1 -> x0, waiting for transfers between devices: 371 us -> none  [body(): lax.psum((stacked[0], stacked[1], stacked[2], stacked[3], stacked[4]), ('...]
    pallas_call x0 -> x1, Pallas kernels: none -> 204 us  [body(): pl.pallas_call(functools.partial(kernel, NW, NZ, R), out_shape=(jax.Shape...]
    all_to_all x7 -> x0, waiting for transfers between devices: 140 us -> none  [the longest x2 52.3 us: body(): lax.all_to_all(lax.all_to_all(forward_shaped, 'wide', split_axis=0, conca...]
    psum x1 -> x0, blocking collectives: 111 us -> none  [body(): lax.psum((stacked[0], stacked[1], stacked[2], stacked[3], stacked[4]), ('...]
    all_to_all x3 -> x0, blocking collectives: 104 us -> none  [the longest x2 69.3 us: body(): lax.all_to_all(shaped, 'wide', split_axis=0, concat_axis=0, tiled=True)]
    all_to_all x7 -> x0, starting transfers between devices: 46.1 us -> none  [the longest x1 14.5 us: body(): lax.all_to_all(totals_grid, 'wide', split_axis=0, concat_axis=0, tiled=True)]
    dot_general x24 -> x0, matrix products: 17.8 us -> none  [the longest x8 5.95 us: left_contract(): lax.dot_general(first, second, (((0,), (0,)), ((), ())), preferred_elemen...]
    gather x2 -> x0, local copies, waits for them, and re-layouts: 9.52 us -> none  [body(): shaped = padded[targets].reshape(wide_count, narrow_count, CAP, width)]
  transfers between devices with their start and end apart: 8 -> 0, of which waited for: 8 -> 0; matrix products, arithmetic and copies ran while one was open for 2% -> 0% of each run, Pallas kernels for 0% -> 0%
where the time goes in v1:
time: 215 us; the launch traced here: 214 us
  Pallas kernels  204 us (95%)
  local copies, waits for them, and re-layouts  9.44 us (4%)
    pallas_call x1, Pallas kernels, body(): pl.pallas_call(functools.partial(kernel, NW, NZ, R), out_shape=(jax.Shape...  204 us
    unnamed x17, local copies, waits for them, and re-layouts  7.23 us

profile of v1, /device:TPU:1, one launch (start us, length us, event | category | flops | bytes accessed | tf_op | source)
XLA Modules:
  0.0 214.4 jit_solution(10767720978198221895)
XLA Ops:
  0.6 0.7 reduce
  1.3 0.3 reshape_squeeze.3
  1.7 0.3 copy.18
  1.9 0.1 copy.17
  2.0 0.8 reshape.20.t_t
  2.9 0.1 copy.19
  2.9 0.6 pad.4.t_y
  3.6 203.5 %shard_map.144 = (bf16[512,256]{1,0:T(8,128)(2,1)}, f32[512,256]{1,0:T(8,128)}, f32[2,256,256]{2,1,0:T(8,128)}, f32[2,256]{1,0:T(2,128)}, f32[2,256,256]{2,1,0:T...) custom-call(bf16[512,256]{1,0:T(8,128)(2,1)} %feat.1, bf16[512,256]{1,0:T(8,128)(2,1)} %ups.1, bf16[1536,512]{1,0:T(8,128)(2,1)} %cnt.1, ...), custom_call_target="tpu_custom_call" | custom-call | flops 12884901888 | bytes 8388608 | tf_op jit(solution)/shard_map/pallas_call | solution.py:473
  207.1 0.0 copy-start.2
  207.1 0.0 copy-start.4
  207.1 0.0 copy-start.1
  207.1 1.8 copy.27
  208.9 0.0 copy-start
  208.9 1.9 copy.28
  210.8 0.0 copy-done.2
  210.8 0.0 copy-start.3
  210.8 0.8 copy.29
  211.6 0.0 copy-done.4
  211.6 0.6 copy.30
  212.2 0.0 copy-done.1
  212.2 0.8 copy.31
  213.0 0.0 copy-done
  213.0 0.8 copy.32
  213.8 0.0 copy-done.3
  213.8 0.6 copy.33
Async XLA Ops:
  207.1 3.7 %copy-start.2 = (f32[2,256,256]{2,1,0:T(8,128)S(1)}, f32[2,256,256]{2,1,0:T(8,128)}, u32[]{:S(2)}) copy-start(f32[2,256,256]{2,1,0:T(8,128)} %get-tuple-element.16) | copy-start | bytes 1572868
  207.1 4.5 %copy-start.4 = (f32[2,256]{1,0:T(2,128)S(1)}, f32[2,256]{1,0:T(2,128)}, u32[]{:S(2)}) copy-start(f32[2,256]{1,0:T(2,128)} %get-tuple-element.17) | copy-start | bytes 6148
  207.1 5.1 %copy-start.1 = (f32[2,256,256]{2,1,0:T(8,128)S(1)}, f32[2,256,256]{2,1,0:T(8,128)}, u32[]{:S(2)}) copy-start(f32[2,256,256]{2,1,0:T(8,128)} %get-tuple-element.18) | copy-start | bytes 1572868
  208.9 4.1 %copy-start = (f32[2,256,256]{2,1,0:T(8,128)S(1)}, f32[2,256,256]{2,1,0:T(8,128)}, u32[]{:S(2)}) copy-start(f32[2,256,256]{2,1,0:T(8,128)} %get-tuple-element.19) | copy-start | bytes 1572868
  210.8 3.0 %copy-start.3 = (f32[2,256]{1,0:T(2,128)S(1)}, f32[2,256]{1,0:T(2,128)}, u32[]{:S(2)}) copy-start(f32[2,256]{1,0:T(2,128)} %get-tuple-element.20) | copy-start | bytes 6148

commit v2 on v1

--- a/solution.py
+++ b/solution.py
@@ -13,6 +13,7 @@
 NC = 2
 GROUP = NX * NC
 EPS = 1e-05
+MATRICES = (2, 3, 1)
 BF = jnp.bfloat16
 F32 = jnp.float32
 MESH = pl.DeviceIdType.MESH
@@ -57,15 +58,14 @@
 
 def kernel(
     NW, NZ, R,
-    feat, ups, cnt, t_n, t_t, t_y, wm, bm, ws, wn, bu,
+    feat_in, ups_in, cnt_in, t_n, wm_in, bm, ws_in, wn_in, bu,
     emb, ing, gm, go, gs, gn, gu,
+    feat, ups, cnt, wm, ws, wn,
     ct, cnt_n, cnt_t, sel_n, sel_t, selt_n, selt_t, m1, m2,
     pre, upre, st, nm, base, low, div,
     sa, za, ma, xa, sb, xb, mb, zb,
     xs, xr, ys, yr,
-    g1s, g1r, g1a, g1b, g1c, g1d, g1e, g1f, g1g,
-    g2s, g2r, g2a, g2b, g2c, g2d, g2e, g2f, g2g,
-    ssem, rsem,
+    *rest,
 ):
     NP = NW // NC
     NY = NP // NX
@@ -129,6 +129,15 @@
     def arrived(dst, slot):
         await_bytes(dst.at[pl.ds(0, dst.shape[0] - 1)], rsem.at[slot])
 
+    groups, (lsem, ssem, rsem) = (rest[:9], rest[9:18], rest[18:27]), rest[27:]
+    loads = [
+        pltpu.make_async_copy(src, dst, lsem.at[k])
+        for k, (src, dst) in enumerate((
+            (cnt_in, cnt), (feat_in, feat), (wm_in, wm), (ws_in, ws), (wn_in, wn), (ups_in, ups)))
+    ]
+    for load in loads:
+        load.start()
+
     barrier = pltpu.get_barrier_semaphore()
 
     def greet(peer, first, last):
@@ -212,75 +221,73 @@
         for k in range(GROUP):
             buf[k, rows:rows + 16, :] = tile.astype(BF)
 
-    def reduce_1(bufs, slot):
-        scatter(bufs[0], bufs[1], slot, q, group_peer, GROUP)
-
-    def reduce_2(bufs, slot):
-        s, r, a = bufs[:3]
-        arrived(r, slot)
-        rows = s.shape[1] - 16
-        piece = rows // NY
+    def reduce_1(g):
+        scatter(groups[g][0], groups[g][1], RED + 5 * g, q, group_peer, GROUP)
+
+    def extra(g):
+        return groups[g][0].shape[1] - 64 * MATRICES[g]
+
+    def reduce_2(g):
+        r, a = groups[g][1], groups[g][2]
+        arrived(r, RED + 5 * g)
+        rows, piece = 64 * MATRICES[g], 64 * MATRICES[g] // NY
         total = r[0].astype(F32)
         for k in range(1, GROUP):
             total = total + r[k].astype(F32)
         for k in range(NY):
-            a[k, 0:piece, :] = total[k * piece:(k + 1) * piece]
-            a[k, piece:piece + 8, :] = total[rows:rows + 8]
-        scatter(a, bufs[3], slot + 1, y, row_peer, NY)
-
-    def reduce_3(bufs, slot):
-        r, s = bufs[3], bufs[4]
-        arrived(r, slot + 1)
-        total = r[0]
+            part = total[k * piece:(k + 1) * piece]
+            if extra(g):
+                part = jnp.concatenate([part, total[rows:rows + 8]], axis=0)
+            a[k] = part.astype(BF)
+        scatter(a, groups[g][3], RED + 5 * g + 1, y, row_peer, NY)
+
+    def reduce_3(g):
+        r, s = groups[g][3], groups[g][4]
+        arrived(r, RED + 5 * g + 1)
+        total = r[0].astype(F32)
         for k in range(1, NY):
-            total = total + r[k]
-        s[...] = total
-        spread_out(s, bufs[5], slot + 2, z, ring_peer, NZ)
-
-    def reduce_4(bufs, slot):
-        r, s = bufs[5], bufs[6]
-        arrived(r, slot + 2)
-        total = r[0]
+            total = total + r[k].astype(F32)
+        s[...] = total.astype(BF)
+        spread_out(s, groups[g][5], RED + 5 * g + 2, z, ring_peer, NZ)
+
+    def reduce_4(g):
+        r, s = groups[g][5], groups[g][6]
+        arrived(r, RED + 5 * g + 2)
+        total = r[0].astype(F32)
         for k in range(1, NZ):
-            total = total + r[k]
-        s[...] = total
-        piece = s.shape[0] - 8
-        src, dst = s.at[pl.ds(0, piece)], bufs[7]
+            total = total + r[k].astype(F32)
+        s[...] = total.astype(BF)
+        spread_out(s, groups[g][7], RED + 5 * g + 3, y, row_peer, NY)
+
+    def reduce_5(g):
+        r, out = groups[g][7], groups[g][8]
+        arrived(r, RED + 5 * g + 3)
+        piece = 64 * MATRICES[g] // NY
+        chunk = jnp.concatenate([r[k].astype(F32)[:piece] for k in range(NY)], axis=0)
+        out[pl.ds(q, 1)] = chunk.astype(BF)[None]
 
         def step(i, _):
-            send(src, dst.at[y], slot + 3, row_peer(NY - i)[1])
-            return _
-        lax.fori_loop(1, NY, step, 0)
-        dst[pl.ds(y, 1)] = s[0:piece][None]
-
-    def reduce_5(bufs, slot):
-        r, out = bufs[7], bufs[8]
-        arrived(r, slot + 3)
-        rows = out.shape[1]
-        out[pl.ds(q, 1)] = r[...].reshape(1, rows, H).astype(BF)
-
-        def step(i, _):
-            send(out.at[q], out.at[q], slot + 4, group_peer(GROUP - i)[1])
+            send(out.at[q], out.at[q], RED + 5 * g + 4, group_peer(GROUP - i)[1])
             return _
         lax.fori_loop(1, GROUP, step, 0)
 
-    def take(bufs, matrix, write):
-        out = bufs[8]
-        for k in range(GROUP):
+    def result(g, targets):
+        out = groups[g][8]
+        arrived(out, RED + 5 * g + 4)
+        for m, (ref, layer) in enumerate(targets):
+            for k in range(GROUP):
+                for h in range(2):
+                    got = out[k, m * 64 + h * 32:m * 64 + (h + 1) * 32, :].astype(F32)
+                    ref[layer, k * 32:(k + 1) * 32, h * H:(h + 1) * H] = got
+
+    def vectors(g, targets):
+        s = groups[g][6]
+        tile = s[s.shape[0] - 16:, :].astype(F32)[8:]
+        for v, (ref, layer) in enumerate(targets):
             for h in range(2):
-                got = out[k, matrix * 64 + h * 32:matrix * 64 + (h + 1) * 32, :].astype(F32)
-                write(slice(k * 32, (k + 1) * 32), slice(h * H, (h + 1) * H), got)
-
-    def take_vector(bufs, index, ref, layer):
-        s = bufs[6]
-        rows = s.shape[0] - 8
-        for h in range(2):
-            ref[layer:layer + 1, h * H:(h + 1) * H] = (
-                s[rows + 2 * index + h:rows + 2 * index + h + 1, :])
-
-    bufs1 = (g1s, g1r, g1a, g1b, g1c, g1d, g1e, g1f, g1g)
-    bufs2 = (g2s, g2r, g2a, g2b, g2c, g2d, g2e, g2f, g2g)
-    TOT, RED1, RED2 = 16, 18, 23
+                ref[layer:layer + 1, h * H:(h + 1) * H] = tile[2 * v + h:2 * v + h + 1, :]
+
+    TOT, RED = 16, 18
 
     def message_half(layer, states):
         value = dot(states, wm[layer]) + bm[layer:layer + 1, :]
@@ -288,9 +295,11 @@
         return (value * sigmoid(value)).astype(BF)
 
     m1[...] = pair_permutation(B)
+    loads[0].wait()
     to_t_order(cnt, ct, R)
-    states = feat[...]
-    st[0] = states
+    loads[1].wait()
+    loads[2].wait()
+    st[0] = feat[...]
     for layer in range(2):
         messages = message_half(layer, st[layer])
         fill_a(layer, ct, messages[:, :H])
@@ -308,6 +317,9 @@
             scatter(xs, xr, TOT, p, plane_peer, NP)
             m2[...] = pair_permutation(NP)
             sel_n[...] = jnp.where(iota((R, S), 0) == t_n[...], 1.0, 0.0).astype(BF)
+            loads[3].wait()
+            loads[4].wait()
+            loads[5].wait()
         base[...] = dot(st[layer], ws[layer]) + bu[layer:layer + 1, :]
         second_b(layer)
         second_a(layer)
@@ -318,26 +330,32 @@
             turned = jnp.zeros((B, H), F32)
             for k in range(2):
                 chosen = jnp.where(lane == 2 * iota((B, H), 0) + k, 1.0, 0.0).astype(BF)
-                put = jnp.where(iota((NP, H), 1) == 2 * iota((NP, H), 0) + k, 1.0, 0.0).astype(BF)
+                put = iota((NP, H), 1) % BR == 2 * iota((NP, H), 0) + k
+                put = jnp.where(put, 1.0, 0.0).astype(BF)
                 turned = turned + dot(dot_nt(chosen, grid).astype(BF), put)
             ys[...] = turned.reshape(B, 1, H)
             scatter(ys, yr, TOT + 1, b, column_peer, B)
-            sel_t[...] = jnp.where(iota((R, S), 0) == t_t[...], 1.0, 0.0).astype(BF)
             selt_n[...] = sel_n[...].T
-            selt_t[...] = sel_t[...].T
+            to_t_order(selt_n, selt_t, R)
+            sel_t[...] = selt_t[...].T
             arrived(yr, TOT + 1)
-
-            def add(k, total):
-                hit = iota((R, H), 0) == t_y[k]
-                return total + jnp.where(hit, yr[k], 0.0)
-            weight = lax.fori_loop(0, B, add, jnp.zeros((R, H), F32))
-            div[...] = jnp.maximum(jnp.sum(weight, axis=1, keepdims=True), 1.0)
+            per = H // BR
+            place_of = iota((1, H), 1) // BR
+            parts = []
+            for k in range(0, B, per):
+                part = yr[k]
+                for j in range(1, per):
+                    part = jnp.where(place_of == j, yr[k + j], part)
+                parts.append(part)
+            row = jnp.broadcast_to(jnp.concatenate(parts, axis=1), (16, S)).astype(BF)
+            weight = dot_nt(sel_t[...], row)
+            div[...] = jnp.maximum(weight[:, 0:1], 1.0)
         else:
             cnt_n[...] = cnt[...].T
             cnt_t[...] = ct[...].T
         divisor = div[...]
+        nm[layer, :, :H] = (dot(sel_n[...], final_a(layer)) / divisor).astype(BF)
         nm[layer, :, H:] = (dot(sel_t[...], final_b(layer)) / divisor).astype(BF)
-        nm[layer, :, :H] = (dot(sel_n[...], final_a(layer)) / divisor).astype(BF)
         value = base[...] + dot(nm[layer], wn[layer])
         upre[layer] = value
         activated = value * sigmoid(value)
@@ -363,55 +381,52 @@
         fill_b(turn, selt_n, spread[:, H:])
         first_b(turn)
         update_grad = jnp.sum(slope, axis=0, keepdims=True)
-        place(g1s, 0 if layer == 1 else 3, dot_tn(st[layer], slope_b))
-        place(g1s, 1 if layer == 1 else 4, dot_tn(nm[layer], slope_b))
-        low[...] = dot_nt(slope_b, ws[layer])
         if layer == 1:
             first_update = update_grad
+            place(groups[0][0], 0, dot_tn(st[1], slope_b))
+            place(groups[0][0], 1, dot_tn(nm[1], slope_b))
+            reduce_1(0)
         else:
-            place_vectors(g1s, 320, (first_update, first_offset, update_grad))
-            reduce_1(bufs1, RED1)
+            first_offset = jnp.sum(base[...], axis=0, keepdims=True)
+            place(groups[1][0], 0, dot_tn(st[1], first_pre_b))
+            place(groups[1][0], 1, dot_tn(st[0], slope_b))
+            place(groups[1][0], 2, dot_tn(nm[0], slope_b))
+            place_vectors(groups[1][0], 192, (first_update, first_offset, update_grad))
+            reduce_1(1)
+            reduce_4(0)
+        low[...] = dot_nt(slope_b, ws[layer])
         second_b(turn)
+        reduce_2(0 if layer == 1 else 1)
         second_a(turn)
-        if layer == 0:
-            reduce_2(bufs1, RED1)
-            reduce_3(bufs1, RED1)
-            reduce_4(bufs1, RED1)
-            reduce_5(bufs1, RED1)
+        if layer == 1:
+            reduce_3(0)
+        else:
+            reduce_3(1)
+            reduce_5(0)
         slope_left = dot(cnt_n[...], final_a(turn))
         slope_right = dot(cnt_t[...], final_b(turn))
         pre_slope = jnp.concatenate([slope_left, slope_right], axis=1) * silu_slope(pre[layer])
         pre_b = pre_slope.astype(BF)
-        offset_grad = jnp.sum(pre_slope, axis=0, keepdims=True)
         if layer == 1:
-            place(g1s, 2, dot_tn(st[1], pre_b))
-            first_offset = offset_grad
             low[...] = low[...] + dot_nt(pre_b, wm[1])
+            base[...] = pre_slope
+            first_pre_b = pre_b
         else:
-            place(g2s, 0, dot_tn(st[0], pre_b))
-            place_vectors(g2s, 64, (offset_grad,))
-            reduce_1(bufs2, RED2)
+            place(groups[2][0], 0, dot_tn(st[0], pre_b))
+            place_vectors(groups[2][0], 64, (jnp.sum(pre_slope, axis=0, keepdims=True),))
+            reduce_1(2)
+            reduce_4(1)
             ing[...] = low[...] + dot_nt(pre_b, wm[0])
-    reduce_2(bufs2, RED2)
-    reduce_3(bufs2, RED2)
-
-    await_bytes(g1g.at[pl.ds(0, GROUP - 1)], rsem.at[RED1 + 4])
-    for matrix, ref, layer in ((0, gs, 1), (1, gn, 1), (2, gm, 1), (3, gs, 0), (4, gn, 0)):
-        def write(rows, columns, got, ref=ref, layer=layer):
-            ref[layer, rows, columns] = got
-        take(bufs1, matrix, write)
-    take_vector(bufs1, 0, gu, 1)
-    take_vector(bufs1, 1, go, 1)
-    take_vector(bufs1, 2, gu, 0)
-
-    reduce_4(bufs2, RED2)
-    reduce_5(bufs2, RED2)
-    await_bytes(g2g.at[pl.ds(0, GROUP - 1)], rsem.at[RED2 + 4])
-
-    def write_last(rows, columns, got):
-        gm[0, rows, columns] = got
-    take(bufs2, 0, write_last)
-    take_vector(bufs2, 0, go, 0)
+    reduce_2(2)
+    reduce_5(1)
+    vectors(1, ((gu, 1), (go, 1), (gu, 0)))
+    reduce_3(2)
+    result(0, ((gs, 1), (gn, 1)))
+    reduce_4(2)
+    result(1, ((gm, 1), (gs, 0), (gn, 0)))
+    vectors(2, ((go, 0),))
+    reduce_5(2)
+    result(2, ((gm, 0),))
 
     for i in range(4):
         await_bytes(sa.at[i, pl.ds(0, B - 1)], ssem.at[4 * i])
@@ -420,40 +435,46 @@
         await_bytes(ma.at[i, pl.ds(0, NP - 1)], ssem.at[4 * i + 3])
     await_bytes(xs.at[pl.ds(0, NP - 1)], ssem.at[TOT])
     await_bytes(ys.at[pl.ds(0, B - 1)], ssem.at[TOT + 1])
-    for bufs, slot in ((bufs1, RED1), (bufs2, RED2)):
-        await_bytes(bufs[1].at[pl.ds(0, GROUP - 1)], ssem.at[slot])
-        await_bytes(bufs[3].at[pl.ds(0, NY - 1)], ssem.at[slot + 1])
-        await_bytes(bufs[5].at[pl.ds(0, NZ - 1)], ssem.at[slot + 2])
-        await_bytes(bufs[7].at[pl.ds(0, NY - 1)], ssem.at[slot + 3])
-        await_bytes(bufs[8].at[pl.ds(0, GROUP - 1)], ssem.at[slot + 4])
+    for g, bufs in enumerate(groups):
+        for stage, (k, n) in enumerate(((1, GROUP), (3, NY), (5, NZ), (7, NY), (8, GROUP))):
+            await_bytes(bufs[k].at[pl.ds(0, n - 1)], ssem.at[RED + 5 * g + stage])
+
+
+def hand_on(*refs):
+    n = len(refs) // 2
+    copies = [
+        pltpu.make_async_copy(refs[k], refs[n + k], refs[-1].at[k]) for k in range(n)]
+    for copy in copies:
+        copy.start()
+    for copy in copies:
+        copy.wait()
 
 
 def body(NW, NZ, features, upstream, visit_counts, target_rows, wm, bm, ws, wn, bu):
     R = features.shape[0]
     S = visit_counts.shape[0]
     NP, B, NY = NW // NC, NC * NZ, NW // GROUP
-    turned = target_rows[0].reshape(NP, B, 2).transpose(1, 0, 2)
-    t_t = turned.reshape(1, S)
-    t_y = jnp.pad(turned.reshape(B, 1, 2 * NP), ((0, 0), (0, 0), (0, H - 2 * NP)), constant_values=R)
-
-    def sum_buffers(matrices):
+
+    def sum_buffers(matrices, extra):
         rows = 64 * matrices
-        piece = rows // NY
+        piece = rows // NY + extra // 2
         return [
-            pltpu.VMEM((GROUP, rows + 16, H), BF),
-            pltpu.VMEM((GROUP, rows + 16, H), BF),
-            pltpu.VMEM((NY, piece + 8, H), F32),
-            pltpu.VMEM((NY, piece + 8, H), F32),
-            pltpu.VMEM((piece + 8, H), F32),
-            pltpu.VMEM((NZ, piece + 8, H), F32),
-            pltpu.VMEM((piece + 8, H), F32),
-            pltpu.VMEM((NY, piece, H), F32),
+            pltpu.VMEM((GROUP, rows + extra, H), BF),
+            pltpu.VMEM((GROUP, rows + extra, H), BF),
+            pltpu.VMEM((NY, piece, H), BF),
+            pltpu.VMEM((NY, piece, H), BF),
+            pltpu.VMEM((piece, H), BF),
+            pltpu.VMEM((NZ, piece, H), BF),
+            pltpu.VMEM((piece, H), BF),
+            pltpu.VMEM((NY, piece, H), BF),
             pltpu.VMEM((GROUP, rows, H), BF),
         ]
 
     column = pltpu.VMEM((4, B, 2 * NP, H), BF)
     plane = pltpu.VMEM((4, NP, 2 * B, H), BF)
     scratch = [
+        pltpu.VMEM((R, F), BF), pltpu.VMEM((R, F), BF), pltpu.VMEM((S, R), BF),
+        pltpu.VMEM((2, F, F), BF), pltpu.VMEM((2, F, F), BF), pltpu.VMEM((2, F, F), BF),
         pltpu.VMEM((S, R), BF), pltpu.VMEM((R, S), BF), pltpu.VMEM((R, S), BF),
         pltpu.VMEM((R, S), BF), pltpu.VMEM((R, S), BF),
         pltpu.VMEM((S, R), BF), pltpu.VMEM((S, R), BF),
@@ -464,25 +485,35 @@
         column, column, plane, plane, plane, plane, column, column,
         pltpu.VMEM((NP, 1, H), F32), pltpu.VMEM((NP, 1, H), F32),
         pltpu.VMEM((B, 1, H), F32), pltpu.VMEM((B, 1, H), F32),
-    ] + sum_buffers(5) + sum_buffers(1) + [
-        pltpu.SemaphoreType.DMA((28,)), pltpu.SemaphoreType.DMA((28,)),
+    ] + sum_buffers(MATRICES[0], 0) + sum_buffers(MATRICES[1], 16) + sum_buffers(MATRICES[2], 16) + [
+        pltpu.SemaphoreType.DMA((6,)), pltpu.SemaphoreType.DMA((33,)), pltpu.SemaphoreType.DMA((33,)),
     ]
     vmem = pl.BlockSpec(memory_space=pltpu.VMEM)
     square = jax.ShapeDtypeStruct((2, F, F), F32)
     line = jax.ShapeDtypeStruct((2, F), F32)
-    return pl.pallas_call(
+    shapes = (
+        jax.ShapeDtypeStruct((R, F), BF), jax.ShapeDtypeStruct((R, F), F32),
+        square, line, square, square, line,
+    )
+    anywhere = pl.BlockSpec(memory_space=pl.ANY)
+    outs = pl.pallas_call(
         functools.partial(kernel, NW, NZ, R),
-        out_shape=(
-            jax.ShapeDtypeStruct((R, F), BF), jax.ShapeDtypeStruct((R, F), F32),
-            square, line, square, square, line,
-        ),
-        in_specs=[vmem] * 11,
+        out_shape=shapes,
+        in_specs=[anywhere, anywhere, anywhere, vmem, anywhere, vmem, anywhere, anywhere, vmem],
         out_specs=[vmem] * 7,
         scratch_shapes=scratch,
         compiler_params=pltpu.CompilerParams(
             collective_id=0, has_side_effects=True, vmem_limit_bytes=58 * 2**20),
         cost_estimate=pl.CostEstimate(flops=12 * 2**30, bytes_accessed=2**23, transcendentals=2**20),
-    )(features, upstream, visit_counts, target_rows, t_t, t_y, wm, bm, ws, wn, bu)
+    )(features, upstream, visit_counts, target_rows, wm, bm, ws, wn, bu)
+    return pl.pallas_call(
+        hand_on,
+        out_shape=shapes,
+        in_specs=[anywhere] * len(shapes),
+        out_specs=[anywhere] * len(shapes),
+        scratch_shapes=[pltpu.SemaphoreType.DMA((len(shapes),))],
+        cost_estimate=pl.CostEstimate(flops=0, bytes_accessed=2**22, transcendentals=0),
+    )(*outs)
 
 
 def solution(mesh):

time: 215 us -> 248 us (1.15)
  Pallas kernels: 204 us -> 247 us
  local copies, waits for them, and re-layouts: 9.44 us -> 0 us
    pallas_call x1 -> x2, Pallas kernels: 204 us -> 247 us  [the longest x1 174 us: body(): pl.pallas_call(functools.partial(kernel, NW, NZ, R), out_shape=shapes, in...]
    unnamed x17 -> x0, local copies, waits for them, and re-layouts: 7.23 us -> none
where the time goes in v2:
time: 248 us; the launch traced here: 247 us
  Pallas kernels  247 us (100%)
    pallas_call x1, Pallas kernels, body(): pl.pallas_call(functools.partial(kernel, NW, NZ, R), out_shape=shapes, in...  174 us
    pallas_call x1, Pallas kernels, body(): pl.pallas_call(hand_on, out_shape=shapes, in_specs=[anywhere] * len(shape...  72.8 us

profile of v2, /device:TPU:1, one launch (start us, length us, event | category | flops | bytes accessed | tf_op | source)
XLA Modules:
  0.0 247.4 jit_solution(10564517480601452117)
XLA Ops:
  0.6 173.9 %shard_map.144 = (bf16[512,256]{1,0:T(8,128)(2,1)}, f32[512,256]{1,0:T(8,128)}, f32[2,256,256]{2,1,0:T(8,128)}, f32[2,256]{1,0:T(2,128)}, f32[2,256,256]{2,1,0:T...) custom-call(bf16[512,256]{1,0:T(8,128)(2,1)} %feat_in.1, bf16[512,256]{1,0:T(8,128)(2,1)} %ups_in.1, ...), custom_call_target="tpu_custom_call" | custom-call | flops 12884901888 | bytes 8388608 | tf_op jit(solution)/shard_map/pallas_call | solution.py:499
  174.5 72.8 %shard_map.145 = (bf16[512,256]{1,0:T(8,128)(2,1)}, f32[512,256]{1,0:T(8,128)}, f32[2,256,256]{2,1,0:T(8,128)}, f32[2,256]{1,0:T(2,128)}, f32[2,256,256]{2,1,0:T...) custom-call(bf16[512,256]{1,0:T(8,128)(2,1)} %get-tuple-element.14.refs_0_, f32[512,256]{1,0:T(8,128)} %get-tuple-element.15.refs_1_, ...), custom_call_target="tpu_custom_call" | custom-call | bytes 4194304 | tf_op jit(solution)/shard_map/pallas_call | solution.py:509

commit v3 on v2

--- a/solution.py
+++ b/solution.py
@@ -23,11 +23,6 @@
     return 1.0 / (1.0 + jnp.exp(-v))
 
 
-def silu_slope(v):
-    sigma = sigmoid(v)
-    return sigma * (1.0 + v * (1.0 - sigma))
-
-
 def dot(a, b):
     return jnp.dot(a, b, preferred_element_type=F32)
 
@@ -62,7 +57,7 @@
     emb, ing, gm, go, gs, gn, gu,
     feat, ups, cnt, wm, ws, wn,
     ct, cnt_n, cnt_t, sel_n, sel_t, selt_n, selt_t, m1, m2,
-    pre, upre, st, nm, base, low, div,
+    dpre, act, dsl, scl, st, st_t, nm, pb, base, low, inv,
     sa, za, ma, xa, sb, xb, mb, zb,
     xs, xr, ys, yr,
     *rest,
@@ -205,12 +200,14 @@
         arrived(zb.at[i], 4 * i + 2)
         return zb[i].reshape(S, H)
 
-    def place(buf, matrix, value):
+    def place_half(buf, matrix, h, value):
         g = value.astype(BF)
         for k in range(GROUP):
-            for h in range(2):
-                buf[k, matrix * 64 + h * 32:matrix * 64 + (h + 1) * 32, :] = (
-                    g[k * 32:(k + 1) * 32, h * H:(h + 1) * H])
+            buf[k, matrix * 64 + h * 32:matrix * 64 + (h + 1) * 32, :] = g[k * 32:(k + 1) * 32]
+
+    def place(buf, matrix, value):
+        for h in range(2):
+            place_half(buf, matrix, h, value[:, h * H:(h + 1) * H])
 
     def place_vectors(buf, rows, vectors):
         tile = jnp.zeros((16, H), F32)
@@ -289,10 +286,19 @@
 
     TOT, RED = 16, 18
 
-    def message_half(layer, states):
-        value = dot(states, wm[layer]) + bm[layer:layer + 1, :]
-        pre[layer] = value
-        return (value * sigmoid(value)).astype(BF)
+    def message_half(layer, half):
+        value = dot(st[layer], wm[layer, :, half]) + bm[layer:layer + 1, half]
+        sigma = sigmoid(value)
+        dpre[layer, :, half] = sigma * (1.0 + value * (1.0 - sigma))
+        return (value * sigma).astype(BF)
+
+    def settle(value):
+        sigma = sigmoid(value)
+        activated = value * sigma
+        scaling = lax.rsqrt(jnp.mean(activated * activated, axis=-1, keepdims=True) + EPS)
+        return activated, sigma * (1.0 + value * (1.0 - sigma)), scaling
+
+    LEFT, RIGHT = slice(0, H), slice(H, F)
 
     m1[...] = pair_permutation(B)
     loads[0].wait()
@@ -301,12 +307,11 @@
     loads[2].wait()
     st[0] = feat[...]
     for layer in range(2):
-        messages = message_half(layer, st[layer])
-        fill_a(layer, ct, messages[:, :H])
+        fill_a(layer, ct, message_half(layer, LEFT))
         if layer == 0:
             pl.semaphore_wait(barrier, NP - 1 + B - 1 + NX - 1)
         first_a(layer)
-        fill_b(layer, cnt, messages[:, H:])
+        fill_b(layer, cnt, message_half(layer, RIGHT))
         first_b(layer)
         if layer == 0:
             totals = jnp.sum(cnt[...].astype(F32), axis=1, keepdims=True).astype(BF)
@@ -349,37 +354,38 @@
                 parts.append(part)
             row = jnp.broadcast_to(jnp.concatenate(parts, axis=1), (16, S)).astype(BF)
             weight = dot_nt(sel_t[...], row)
-            div[...] = jnp.maximum(weight[:, 0:1], 1.0)
+            inv[...] = 1.0 / jnp.maximum(weight[:, 0:1], 1.0)
+            st_t[...] = st[0].T
         else:
             cnt_n[...] = cnt[...].T
             cnt_t[...] = ct[...].T
-        divisor = div[...]
-        nm[layer, :, :H] = (dot(sel_n[...], final_a(layer)) / divisor).astype(BF)
-        nm[layer, :, H:] = (dot(sel_t[...], final_b(layer)) / divisor).astype(BF)
-        value = base[...] + dot(nm[layer], wn[layer])
-        upre[layer] = value
-        activated = value * sigmoid(value)
-        scaling = lax.rsqrt(jnp.mean(activated * activated, axis=-1, keepdims=True) + EPS)
-        states = (activated * scaling).astype(BF)
+        left = (dot(sel_n[...], final_a(layer)) * inv[...]).astype(BF)
+        nm[layer, :, LEFT] = left
+        partial = base[...] + dot(left, wn[layer, LEFT, :])
+        right = (dot(sel_t[...], final_b(layer)) * inv[...]).astype(BF)
+        nm[layer, :, RIGHT] = right
+        activated, steep, scaling = settle(partial + dot(right, wn[layer, RIGHT, :]))
         if layer == 0:
-            st[1] = states
+            st[1] = (activated * scaling).astype(BF)
+            act[...] = activated
+            dsl[...] = steep
+            scl[...] = scaling
+
+    for turn, layer in ((2, 1), (3, 0)):
+        if layer == 1:
+            upward = ups[...].astype(F32)
+            states = (activated * scaling).astype(BF)
         else:
+            upward, activated, steep, scaling = low[...], act[...], dsl[...], scl[...]
+        inner = jnp.mean(upward * activated, axis=-1, keepdims=True)
+        slope = (scaling * upward - activated * ((scaling * scaling * scaling) * inner)) * steep
+        slope_b = slope.astype(BF)
+        fill_a(turn, selt_t, (dot_nt(slope_b, wn[layer, LEFT, :]) * inv[...]).astype(BF))
+        first_a(turn)
+        fill_b(turn, selt_n, (dot_nt(slope_b, wn[layer, RIGHT, :]) * inv[...]).astype(BF))
+        first_b(turn)
+        if layer == 1:
             emb[...] = states
-
-    for turn, layer in ((2, 1), (3, 0)):
-        upward = ups[...].astype(F32) if layer == 1 else low[...]
-        value = upre[layer]
-        activated = value * sigmoid(value)
-        scaling = lax.rsqrt(jnp.mean(activated * activated, axis=-1, keepdims=True) + EPS)
-        inner = jnp.mean(upward * activated, axis=-1, keepdims=True)
-        slope = scaling * upward - activated * (scaling * scaling * scaling) * inner
-        slope = slope * silu_slope(value)
-        slope_b = slope.astype(BF)
-        spread = (dot_nt(slope_b, wn[layer]) / div[...]).astype(BF)
-        fill_a(turn, selt_t, spread[:, :H])
-        first_a(turn)
-        fill_b(turn, selt_n, spread[:, H:])
-        first_b(turn)
         update_grad = jnp.sum(slope, axis=0, keepdims=True)
         if layer == 1:
             first_update = update_grad
@@ -388,8 +394,8 @@
             reduce_1(0)
         else:
             first_offset = jnp.sum(base[...], axis=0, keepdims=True)
-            place(groups[1][0], 0, dot_tn(st[1], first_pre_b))
-            place(groups[1][0], 1, dot_tn(st[0], slope_b))
+            place(groups[1][0], 0, dot_tn(st[1], pb[...]))
+            place(groups[1][0], 1, dot(st_t[...], slope_b))
             place(groups[1][0], 2, dot_tn(nm[0], slope_b))
             place_vectors(groups[1][0], 192, (first_update, first_offset, update_grad))
             reduce_1(1)
@@ -403,20 +409,20 @@
         else:
             reduce_3(1)
             reduce_5(0)
-        slope_left = dot(cnt_n[...], final_a(turn))
-        slope_right = dot(cnt_t[...], final_b(turn))
-        pre_slope = jnp.concatenate([slope_left, slope_right], axis=1) * silu_slope(pre[layer])
-        pre_b = pre_slope.astype(BF)
-        if layer == 1:
-            low[...] = low[...] + dot_nt(pre_b, wm[1])
-            base[...] = pre_slope
-            first_pre_b = pre_b
-        else:
-            place(groups[2][0], 0, dot_tn(st[0], pre_b))
-            place_vectors(groups[2][0], 64, (jnp.sum(pre_slope, axis=0, keepdims=True),))
+        for half, incoming, counts in ((LEFT, final_a, cnt_n), (RIGHT, final_b, cnt_t)):
+            pre_slope = dot(counts[...], incoming(turn)) * dpre[layer, :, half]
+            pre_b = pre_slope.astype(BF)
+            base[:, half] = pre_slope
+            pb[:, half] = pre_b
+            if layer == 1:
+                low[...] += dot_nt(pre_b, wm[1, :, half])
+            else:
+                place_half(groups[2][0], 0, half.start // H, dot(st_t[...], pre_b))
+        if layer == 0:
+            place_vectors(groups[2][0], 64, (jnp.sum(base[...], axis=0, keepdims=True),))
             reduce_1(2)
             reduce_4(1)
-            ing[...] = low[...] + dot_nt(pre_b, wm[0])
+            ing[...] = low[...] + dot_nt(pb[...], wm[0])
     reduce_2(2)
     reduce_5(1)
     vectors(1, ((gu, 1), (go, 1), (gu, 0)))
@@ -442,12 +448,8 @@
 
 def hand_on(*refs):
     n = len(refs) // 2
-    copies = [
-        pltpu.make_async_copy(refs[k], refs[n + k], refs[-1].at[k]) for k in range(n)]
-    for copy in copies:
-        copy.start()
-    for copy in copies:
-        copy.wait()
+    for k in range(n):
+        refs[n + k][...] = refs[k][...]
 
 
 def body(NW, NZ, features, upstream, visit_counts, target_rows, wm, bm, ws, wn, bu):
@@ -479,8 +481,8 @@
         pltpu.VMEM((R, S), BF), pltpu.VMEM((R, S), BF),
         pltpu.VMEM((S, R), BF), pltpu.VMEM((S, R), BF),
         pltpu.VMEM((16 * B, 16 * B), BF), pltpu.VMEM((16 * NP, 16 * NP), BF),
-        pltpu.VMEM((2, R, F), F32), pltpu.VMEM((2, R, F), F32),
-        pltpu.VMEM((2, R, F), BF), pltpu.VMEM((2, R, F), BF),
+        pltpu.VMEM((2, R, F), F32), pltpu.VMEM((R, F), F32), pltpu.VMEM((R, F), F32), pltpu.VMEM((R, 1), F32),
+        pltpu.VMEM((2, R, F), BF), pltpu.VMEM((F, R), BF), pltpu.VMEM((2, R, F), BF), pltpu.VMEM((R, F), BF),
         pltpu.VMEM((R, F), F32), pltpu.VMEM((R, F), F32), pltpu.VMEM((R, 1), F32),
         column, column, plane, plane, plane, plane, column, column,
         pltpu.VMEM((NP, 1, H), F32), pltpu.VMEM((NP, 1, H), F32),
@@ -509,9 +511,9 @@
     return pl.pallas_call(
         hand_on,
         out_shape=shapes,
-        in_specs=[anywhere] * len(shapes),
-        out_specs=[anywhere] * len(shapes),
-        scratch_shapes=[pltpu.SemaphoreType.DMA((len(shapes),))],
+        in_specs=[vmem] * len(shapes),
+        out_specs=[vmem] * len(shapes),
+        compiler_params=pltpu.CompilerParams(vmem_limit_bytes=16 * 2**20),
         cost_estimate=pl.CostEstimate(flops=0, bytes_accessed=2**22, transcendentals=0),
     )(*outs)
 

time: 248 us -> 183 us (0.74)
  Pallas kernels: 247 us -> 176 us
  local copies, waits for them, and re-layouts: 0 us -> 6.46 us
    pallas_call x1, Pallas kernels: 72.8 us -> 1.55 us  [body(): pl.pallas_call(hand_on, out_shape=shapes, in_specs=[vmem] * len(shapes),...]
    unnamed x0 -> x14, local copies, waits for them, and re-layouts: none -> 6.46 us
where the time goes in v3:
time: 183 us
  Pallas kernels  176 us (96%)
  local copies, waits for them, and re-layouts  6.46 us (4%)
    pallas_call x1, Pallas kernels, body(): pl.pallas_call(functools.partial(kernel, NW, NZ, R), out_shape=shapes, in...  174 us
    unnamed x14, local copies, waits for them, and re-layouts  6.46 us

profile of v3, /device:TPU:1, one launch (start us, length us, event | category | flops | bytes accessed | tf_op | source)
XLA Modules:
  0.0 182.7 jit_solution(14972698955560862100)
XLA Ops:
  0.6 174.1 %shard_map.144 = (bf16[512,256]{1,0:T(8,128)(2,1)}, f32[512,256]{1,0:T(8,128)}, f32[2,256,256]{2,1,0:T(8,128)}, f32[2,256]{1,0:T(2,128)}, f32[2,256,256]{2,1,0:T...) custom-call(bf16[512,256]{1,0:T(8,128)(2,1)} %feat_in.1, bf16[512,256]{1,0:T(8,128)(2,1)} %ups_in.1, ...), custom_call_target="tpu_custom_call" | custom-call | flops 12884901888 | bytes 8388608 | tf_op jit(solution)/shard_map/pallas_call | solution.py:501
  174.7 0.0 copy-start
  174.7 1.0 copy-done
  175.8 0.0 copy-start.1
  175.8 1.0 copy-done.1
  176.8 0.0 copy-start.2
  176.8 1.0 copy-done.2
  177.8 0.0 copy-start.3
  177.8 1.0 copy-done.3
  178.9 0.0 copy-start.4
  178.9 0.9 copy-done.4
  179.8 0.0 copy-start.5
  179.8 0.7 copy-done.5
  180.5 0.0 copy-start.6
  180.5 0.7 copy-done.6
  181.2 1.6 shard_map.145
Async XLA Ops:
  174.7 1.0 copy-start
  175.8 1.0 copy-start.1
  176.8 1.0 copy-start.2
  177.8 1.0 copy-start.3
  178.9 0.9 copy-start.4
  179.8 0.7 copy-start.5
  180.5 0.7 copy-start.6

commit v4 on v3

--- a/solution.py
+++ b/solution.py
@@ -429,9 +429,9 @@
     reduce_3(2)
     result(0, ((gs, 1), (gn, 1)))
     reduce_4(2)
-    result(1, ((gm, 1), (gs, 0), (gn, 0)))
     vectors(2, ((go, 0),))
     reduce_5(2)
+    result(1, ((gm, 1), (gs, 0), (gn, 0)))
     result(2, ((gm, 0),))
 
     for i in range(4):
@@ -447,9 +447,17 @@
 
 
 def hand_on(*refs):
-    n = len(refs) // 2
-    for k in range(n):
-        refs[n + k][...] = refs[k][...]
+    n = (len(refs) - 2) // 3
+    sources, outs, held, (in_sem, out_sem) = refs[:n], refs[n:2 * n], refs[2 * n:3 * n], refs[3 * n:]
+    reads = [pltpu.make_async_copy(sources[k], held[k], in_sem.at[k]) for k in range(n)]
+    writes = [pltpu.make_async_copy(held[k], outs[k], out_sem.at[k]) for k in range(n)]
+    for read in reads:
+        read.start()
+    for read, write in zip(reads, writes):
+        read.wait()
+        write.start()
+    for write in writes:
+        write.wait()
 
 
 def body(NW, NZ, features, upstream, visit_counts, target_rows, wm, bm, ws, wn, bu):
@@ -511,9 +519,12 @@
     return pl.pallas_call(
         hand_on,
         out_shape=shapes,
-        in_specs=[vmem] * len(shapes),
-        out_specs=[vmem] * len(shapes),
-        compiler_params=pltpu.CompilerParams(vmem_limit_bytes=16 * 2**20),
+        in_specs=[anywhere] * len(shapes),
+        out_specs=[anywhere] * len(shapes),
+        scratch_shapes=[pltpu.VMEM(shape.shape, shape.dtype) for shape in shapes] + [
+            pltpu.SemaphoreType.DMA((len(shapes),)), pltpu.SemaphoreType.DMA((len(shapes),)),
+        ],
+        compiler_params=pltpu.CompilerParams(vmem_limit_bytes=60 * 2**20),
         cost_estimate=pl.CostEstimate(flops=0, bytes_accessed=2**22, transcendentals=0),
     )(*outs)
 

time: 183 us -> 178 us (0.973)
  local copies, waits for them, and re-layouts: 6.46 us -> 0 us
    unnamed x14 -> x0, local copies, waits for them, and re-layouts: 6.46 us -> none
where the time goes in v4:
time: 178 us; the launch traced here: 177 us
  Pallas kernels  177 us (99%)
    pallas_call x1, Pallas kernels, body(): pl.pallas_call(functools.partial(kernel, NW, NZ, R), out_shape=shapes, in...  174 us

profile of v4, /device:TPU:1, one launch (start us, length us, event | category | flops | bytes accessed | tf_op | source)
XLA Modules:
  0.0 177.5 jit_solution(2411283223422689103)
XLA Ops:
  0.6 174.1 %shard_map.144 = (bf16[512,256]{1,0:T(8,128)(2,1)}, f32[512,256]{1,0:T(8,128)}, f32[2,256,256]{2,1,0:T(8,128)}, f32[2,256]{1,0:T(2,128)}, f32[2,256,256]{2,1,0:T...) custom-call(bf16[512,256]{1,0:T(8,128)(2,1)} %feat_in.1, bf16[512,256]{1,0:T(8,128)(2,1)} %ups_in.1, ...), custom_call_target="tpu_custom_call" | custom-call | flops 12884901888 | bytes 8388608 | tf_op jit(solution)/shard_map/pallas_call | solution.py:509
  174.7 2.6 %shard_map.145 = (bf16[512,256]{1,0:T(8,128)(2,1)}, f32[512,256]{1,0:T(8,128)}, f32[2,256,256]{2,1,0:T(8,128)}, f32[2,256]{1,0:T(2,128)}, f32[2,256,256]{2,1,0:T...) custom-call(bf16[512,256]{1,0:T(8,128)(2,1)} %get-tuple-element.14.refs_0_, f32[512,256]{1,0:T(8,128)} %get-tuple-element.15.refs_1_, ...), custom_call_target="tpu_custom_call" | custom-call | bytes 4194304 | tf_op jit(solution)/shard_map/pallas_call | solution.py:519
